TPU v7x, 256 devices: a whole 4x4x8 slice. The times are simulated.
256 devices in a mesh: section: 16 (over z, x_hi), tensor: 16 (over x_lo, y, core).
Axes of the slice: x: 4 (x_hi: 2, x_lo: 2; x = x_hi * 2 + x_lo), y: 4, z: 8, core: 2. Of those that a mesh axis runs over, the one named last changes fastest.
Arguments:
- old_weight: float32 [16, 256, 6144], P('section', 'tensor'), may hold values from -6 to 6
- old_first: float32 [16, 256, 6144], P('section', 'tensor'), may hold values from -6 to 6
- old_second: float32 [16, 256, 6144], P('section', 'tensor'), may hold values from 0.1 to 2
- mixing: float32 [32, 16], replicated, may hold values from -1.5 to 1.5
- target_rms: float32 [32], P('section'), may hold values from 0.5 to 2
Outputs:
- new_weight: float32 [32, 256, 6144], P('section', 'tensor')
- new_first: float32 [32, 256, 6144], P('section', 'tensor')
- new_second: float32 [32, 256, 6144], P('section', 'tensor')
All inputs are finite; a program needn't handle non-finite values.
Results may differ from a plain program's by a relative error of at most 0.0003.
Values sent between devices are 32-bit elements; how exact they have to be, the bound alone decides.
A program may use at most 192 MiB of HBM per device.

v0:
```python
import jax
import jax.numpy as jnp
from jax import lax
from jax.sharding import PartitionSpec as P


def apply_coefs(coefs, stack):
    return jnp.einsum(
        "nl,lrd->nrd",
        coefs,
        stack,
        precision=lax.Precision.HIGHEST,
        preferred_element_type=jnp.float32,
    )


def local(old_weight, old_first, old_second, mixing, target_rms):
    new_count = target_rms.shape[0]
    row_count = old_weight.shape[1]
    width = old_weight.shape[2]
    first_new = lax.axis_index("section") * new_count
    my_coefs = lax.dynamic_slice_in_dim(mixing, first_new, new_count, 0)
    mixed_weight = apply_coefs(my_coefs, lax.all_gather(old_weight, "section", axis=0, tiled=True))
    mixed_first = apply_coefs(my_coefs, lax.all_gather(old_first, "section", axis=0, tiled=True))
    mixed_second = apply_coefs(
        my_coefs * my_coefs, lax.all_gather(old_second, "section", axis=0, tiled=True)
    )
    local_power = jnp.sum(mixed_weight * mixed_weight, axis=(1, 2))
    power = lax.psum(local_power, "tensor")
    total_rows = row_count * lax.axis_size("tensor")
    factor = target_rms / jnp.sqrt(power / (total_rows * width) + 1e-06)
    scale = factor[:, None, None]
    return (scale * mixed_weight, scale * mixed_first, scale * scale * mixed_second)


def solution(mesh):
    return jax.shard_map(
        local,
        mesh=mesh,
        in_specs=(
            P("section", "tensor", None),
            P("section", "tensor", None),
            P("section", "tensor", None),
            P(),
            P("section"),
        ),
        out_specs=(
            P("section", "tensor", None),
            P("section", "tensor", None),
            P("section", "tensor", None),
        ),
        check_vma=False,
    )
```

profile of v0, /device:TPU:2, one launch (start us, length us, event | category | flops | bytes accessed | tf_op | source)
XLA Modules:
  0.0 376.7 jit_solution(11940619525149013062)
XLA Ops:
  7.2 0.0 copy-start
  7.2 0.0 copy-start.1
  7.2 0.0 all-gather.4.cloned.1.call-start
  7.2 0.7 all-gather.4.cloned.1.call-update
  7.9 0.0 all-gather.6.cloned.1.call-start
  8.0 0.7 all-gather.6.cloned.1.call-update
  8.7 0.0 all-gather.8.cloned.1.call-start
  8.7 0.7 all-gather.8.cloned.1.call-update
  9.4 0.8 dynamic-slice_multiply_fusion
  10.2 0.1 copy.23
  10.3 118.2 %all-gather.4.cloned.1.call-done = f32[16,16,6144]{2,1,0:T(8,128)} async-done(((f32[1,16,6144]{2,1,0:T(8,128)}), f32[16,16,6144]{2,1,0:T(8,128)}) %all-gather.4.cloned.1.call-update) | async-done | bytes 6291472 | tf_op jit(solution)/shard_map/all_gather | solution.py:23
  128.5 10.2 %multiply_reduce_fusion = (f32[2]{0:T(128)S(1)}, f32[2,16,6144]{2,0,1:T(2,128)S(1)}) fusion(f32[16,16,6144]{2,1,0:T(8,128)} %all-gather.4.cloned.1.call-done, f32[32,16]{0,1:T(8,128)} %param.8, s32[]{:T(128)S(6)} %select_n.3), kind=kOutput, calls=%fused_computation.6 | convolution fusion | flops 38141952 | bytes 7079948 | tf_op jit(solution)/shard_map/nl,lrd->nrd/dot_general | solution.py:8
  138.7 29.6 %psum.7 = f32[2]{0:T(128)S(1)} all-reduce(f32[2]{0:T(128)S(1)} %get-tuple-element.11), channel_id=1, replica_groups=mesh['section'=16,'tensor'=16] {'tensor'}, use_global_device_ids=true, to_apply=%region_1.0 | all-reduce | flops 2 | bytes 16 | tf_op jit(solution)/shard_map/psum | solution.py:29
  168.3 0.0 copy-done.1
  168.3 0.4 broadcast_multiply_fusion
  168.7 1.3 copy.19
  170.0 73.8 %all-gather.6.cloned.1.call-done = f32[16,16,6144]{2,1,0:T(8,128)} async-done(((f32[1,16,6144]{2,1,0:T(8,128)}), f32[16,16,6144]{2,1,0:T(8,128)}) %all-gather.6.cloned.1.call-update) | async-done | bytes 6291472 | tf_op jit(solution)/shard_map/all_gather | solution.py:24
  243.8 0.0 copy-done
  243.8 9.7 %convolution_multiply_fusion.1 = f32[2,16,6144]{2,0,1:T(2,128)S(1)} fusion(f32[16,16,6144]{2,1,0:T(8,128)} %all-gather.6.cloned.1.call-done, f32[2]{0:T(128)S(1)} %get-tuple-element.10, f32[32,16]{0,1:T(8,128)S(1)} %copy-done, s32[]{:T(128)S(6)} %select_n.3), kind=kOutput, calls=%fused_computation.1 | convolution fusion | flops 37945344 | bytes 7079948 | tf_op jit(solution)/shard_map/nl,lrd->nrd/dot_general | solution.py:8
  253.5 1.3 copy.20
  254.8 104.3 %all-gather.8.cloned.1.call-done = f32[16,16,6144]{2,1,0:T(8,128)} async-done(((f32[1,16,6144]{2,1,0:T(8,128)}), f32[16,16,6144]{2,1,0:T(8,128)}) %all-gather.8.cloned.1.call-update) | async-done | bytes 6291472 | tf_op jit(solution)/shard_map/all_gather | solution.py:26
  359.2 9.6 %convolution_multiply_fusion = f32[2,16,6144]{2,0,1:T(2,128)S(1)} fusion(f32[16,16,6144]{2,1,0:T(8,128)} %all-gather.8.cloned.1.call-done, f32[2]{0:T(128)S(1)} %get-tuple-element.9, f32[2,16]{1,0:T(2,128)S(1)} %copy.23), kind=kOutput, calls=%fused_computation | convolution fusion | flops 37945344 | bytes 7078024 | tf_op jit(solution)/shard_map/nl,lrd->nrd/dot_general | solution.py:8
  368.8 1.3 copy.21
  (1 shorter events, 0.0 us)
Async XLA Ops:
  7.2 236.7 %copy-start = (f32[32,16]{0,1:T(8,128)S(1)}, f32[32,16]{0,1:T(8,128)}, u32[]{:S(2)}) copy-start(f32[32,16]{0,1:T(8,128)} %param.8) | copy-start | bytes 6148
  7.2 161.1 %copy-start.1 = (f32[2]{0:T(128)S(1)}, f32[2]{0:T(128)}, u32[]{:S(2)}) copy-start(f32[2]{0:T(128)} %param.9) | copy-start | bytes 28
  7.2 121.3 %all-gather.4.cloned.1.call-start = ((), (), s32[]{:S(2)}) async-start(), calls=%async_computation | async-start | bytes 6684672 | tf_op jit(solution)/shard_map/all_gather | solution.py:23
  7.9 235.9 %all-gather.6.cloned.1.call-start = ((), (), s32[]{:S(2)}) async-start(), calls=%async_computation.1 | async-start | bytes 6684672 | tf_op jit(solution)/shard_map/all_gather | solution.py:24
  8.7 350.5 %all-gather.8.cloned.1.call-start = ((), (), s32[]{:S(2)}) async-start(), calls=%async_computation.2 | async-start | bytes 6684672 | tf_op jit(solution)/shard_map/all_gather | solution.py:26
Sparse Core Ops, SparseCore 0:
  10.6 117.8 all-gather.3
  131.1 112.7 all-gather.5
  246.4 112.7 all-gather.7
where the time goes:
time: 378 us; the launch traced here: 377 us
  waiting for transfers between devices  298 us (79%)
  blocking collectives  29.6 us (8%)
  matrix products  29.5 us (8%)
  between operations  13.8 us (4%)
  local copies, waits for them, and re-layouts  4.11 us (1%)
    all_gather x1, waiting for transfers between devices, local(): lax.all_gather(old_weight, 'section', axis=0, tiled=True)  118 us
    all_gather x1, waiting for transfers between devices, local(): lax.all_gather(old_second, 'section', axis=0, tiled=True)  104 us
    all_gather x1, waiting for transfers between devices, local(): lax.all_gather(old_first, 'section', axis=0, tiled=True)  73.8 us
    psum x1, blocking collectives, local(): power = lax.psum(local_power, 'tensor')  29.6 us
    dot_general x3, matrix products, apply_coefs(): jnp.einsum('nl,lrd->nrd', coefs, stack, precision=lax.Precision.HIGHEST,...  29.5 us
  transfers between devices with their start and end apart: 3, of which 3 were waited for; matrix products, arithmetic and copies ran while one was open for 6% of the time, Pallas kernels for 0%

commit v1 on v0

v1 whole, which is shorter than its diff:
```python
import jax
import jax.numpy as jnp
from jax import lax
from jax.experimental import pallas as pl
from jax.experimental.pallas import tpu as pltpu
from jax.sharding import PartitionSpec as P

MESH = pl.DeviceIdType.MESH
F32 = jnp.float32

PLANES = 8
LANES = 128
CHUNK = 1024
ROLES = (5, 4, 3, 2, 1, 0, 7, 6)

SOURCES = {
    0: (("own", 5, 0), ("r1", 3, -1), ("r1", 4, -2), ("l1", 4, 1), ("l2", 3, 2), ("l3", 2, 3), ("l4", 1, 4), ("l4", 0, 5)),
    1: (("own", 4, 0), ("r1", 2, -1), ("r2", 2, -2), ("r2", 3, -3), ("l1", 3, 1), ("l2", 2, 2), ("l3", 1, 3), ("l3", 0, 4)),
    2: (("own", 3, 0), ("r1", 1, -1), ("r2", 1, -2), ("r3", 1, -3), ("r3", 2, -4), ("l1", 2, 1), ("l2", 1, 2), ("l2", 0, 3)),
    3: (("own", 2, 0), ("r1", 0, -1), ("r2", 0, -2), ("r3", 0, -3), ("r4", 0, -4), ("r4", 1, -5), ("l1", 1, 1), ("l1", 0, 2)),
}
TARGETS = {0: ((-2, 0), (-1, 2), (0, 4)), 3: ((2, 1), (1, 3), (0, 5)), 1: ((0, 6),), 2: ((0, 7),)}
FORWARD = {
    2: (("r1", 1, "r2", 4, 1), ("l1", 0, "l2", 4, -1)),
    3: (("r2", 1, "r3", 3, 1), ("l2", 0, "l3", 3, -1)),
    4: (("r3", 1, "r4", 2, 1), ("l3", 0, "l4", 2, -1)),
}
LEAD = 3
LAG = {2: 1, 3: 2, 4: 3, "mix": 4, "join": 5, "end": 6}


def kernel(weight, first, second, mixing, target, mixed, factor, stage, own, r1, r2, r3, r4, l1, l2, l3, l4,
           part, sent, came, back, done, pow_sent, pow_came, in_sem, out_sem, ssem, rsem, pow_ssem, pow_rsem):
    count = own.shape[0]
    per = count // 3
    width = own.shape[3]
    rows = own.shape[2]
    section = lax.axis_index("section")
    tensor = lax.axis_index("tensor")
    z = section // 2
    half = lax.rem(section, 2)
    refs = dict(own=own, r1=r1, r2=r2, r3=r3, r4=r4, l1=l1, l2=l2, l3=l3, l4=l4)

    def plane(step):
        return lax.rem(z + (step + PLANES), PLANES)

    def along(step):
        return (plane(step) * 2 + half, tensor)

    def flip(bit):
        return (section, tensor + bit - 2 * bit * lax.rem(tensor // bit, 2))

    across = (z * 2 + 1 - half, tensor)
    bits = (1, 8, 2, 4)
    partners = [flip(bit) for bit in bits]

    loads = []
    for a, array in enumerate((weight, first, second)):
        for s in range(per):
            c = a * per + s
            loads.append(pltpu.make_async_copy(
                array.at[0, :, pl.ds(s * CHUNK, CHUNK)], stage.at[c], in_sem.at[c]))
    for load in loads:
        load.start()

    barrier = pltpu.get_barrier_semaphore()
    peers = [along(1), along(-1), along(2), along(-2), across] + partners
    for peer in peers:
        pl.semaphore_signal(barrier, inc=1, device_id=peer, device_id_type=MESH)

    for load in loads:
        load.wait()

    def turn(c, _):
        for i in range(PLANES):
            slab = lax.rem(z + (i + 3), PLANES)
            own[c, i] = stage[c, :, pl.ds(pl.multiple_of(slab * width, LANES), width)]
        return 0

    lax.fori_loop(0, count, turn, 0)
    pl.semaphore_wait(barrier, len(peers))

    def remote(src, dst, c, k, device):
        return pltpu.make_async_remote_copy(
            src_ref=src, dst_ref=dst, send_sem=ssem.at[c, k], recv_sem=rsem.at[c, k],
            device_id=device, device_id_type=MESH)

    def step1(c):
        return [
            remote(own.at[c, pl.ds(3, 4)], r1.at[c, pl.ds(0, 4)], c, 0, along(1)),
            remote(own.at[c, pl.ds(7, 1)], r1.at[c, pl.ds(4, 1)], c, 1, along(2)),
            remote(own.at[c, pl.ds(1, 4)], l1.at[c, pl.ds(1, 4)], c, 2, along(-1)),
            remote(own.at[c, pl.ds(0, 1)], l1.at[c, pl.ds(0, 1)], c, 3, along(-2)),
        ]

    def forward(k, c):
        return [
            remote(refs[src].at[c, pl.ds(at, n)], refs[dst].at[c, pl.ds(0, n)], c, 2 * k + i, along(way))
            for i, (src, at, dst, n, way) in enumerate(FORWARD[k])
        ]

    def cross(c):
        return [
            remote(sent.at[c, pl.ds(0, 4)], came.at[c, pl.ds(0, 4)], c, 10, across),
            remote(sent.at[c, pl.ds(4, 2)], came.at[c, pl.ds(4, 2)], c, 11, across),
            remote(sent.at[c, pl.ds(6, 2)], came.at[c, pl.ds(6, 2)], c, 12, across),
        ]

    def give(c):
        return [
            remote(part.at[c, i], back.at[c, i], c, 13 + i, along(way))
            for i, way in enumerate((-2, 2, -1, 1))
        ]

    def mix(c, role):
        squared = c >= 2 * per
        for step, place in TARGETS[role]:
            to = plane(step) * 2
            for lane in range(0, width, LANES):
                lanes = pl.ds(lane, LANES)
                sums = [[None, None], [None, None]]
                for name, at, away in SOURCES[role]:
                    old = refs[name][c, at, :, lanes]
                    layer = plane(away) * 2 + half
                    for other in range(2):
                        to_half = 1 - half if other else half
                        for n in range(2):
                            coef = mixing[2 * (to + to_half) + n, layer]
                            coef = coef * jnp.where(squared, coef, 1.0)
                            term = coef * old
                            sums[other][n] = term if sums[other][n] is None else sums[other][n] + term
                for n in range(2):
                    part[c, place, n, :, lanes] = sums[0][n]
                    sent[c, place, n, :, lanes] = sums[1][n]

    def output(c):
        s = lax.rem(c, per)
        return pltpu.make_async_copy(
            done.at[c], mixed.at[c // per, :, :, pl.ds(pl.multiple_of(s * CHUNK, CHUNK), CHUNK)], out_sem.at[c])

    def finish(c):
        for role in range(PLANES):
            slab = lax.rem(z + (PLANES - role), PLANES)
            lanes = pl.ds(pl.multiple_of(slab * width, LANES), width)
            ref, at = {0: (part, 4), 1: (part, 6), 2: (part, 7), 3: (part, 5),
                       4: (back, 3), 5: (back, 1), 6: (back, 0), 7: (back, 2)}[role]
            done[c, :, :, lanes] = ref[c, at]

    def power(c):
        for n in range(2):
            total = pow_sent[0, n]
            for lane in range(0, CHUNK, LANES):
                for row in range(0, rows, 8):
                    value = done[c, n, pl.ds(row, 8), pl.ds(lane, LANES)]
                    total = total + value * value
            pow_sent[0, n] = total

    def pow_copy(k):
        return pltpu.make_async_remote_copy(
            src_ref=pow_sent.at[k], dst_ref=pow_came.at[k], send_sem=pow_ssem.at[k], recv_sem=pow_rsem.at[k],
            device_id=partners[k], device_id_type=MESH)

    pow_sent[0] = jnp.zeros_like(pow_sent[0])
    for c in range(LEAD):
        for copy in step1(c):
            copy.start()

    pow_turn = LAG["end"] + per - 1

    def turn_of(t, _):
        def at(lag, body):
            c = t - lag

            @pl.when((c >= 0) & (c < count))
            def _():
                body(c)

        def do_end(c):
            for copy in give(c):
                copy.wait()
            finish(c)
            output(c).start()

            @pl.when(c < per)
            def _():
                power(c)

        def do_join(c):
            for copy in cross(c):
                copy.wait()
            for i in range(8):
                part[c, i] = part[c, i] + came[c, i]
            for copy in give(c):
                copy.start()

        def do_mix(c):
            for copy in forward(4, c):
                copy.wait()
            for role in (0, 3):
                mix(c, role)
            copies = cross(c)
            copies[0].start()
            copies[1].start()
            for role in (1, 2):
                mix(c, role)
            copies[2].start()

        def do_forward(k, c):
            before = step1(c) if k == 2 else forward(k - 1, c)
            for copy in before:
                copy.wait()
            for copy in forward(k, c):
                copy.start()

        def do_first(c):
            for copy in step1(c):
                copy.start()

        at(LAG["end"], do_end)
        at(LAG["join"], do_join)
        at(LAG[4], lambda c: do_forward(4, c))
        at(LAG[3], lambda c: do_forward(3, c))
        at(LAG[2], lambda c: do_forward(2, c))
        at(-LEAD, do_first)
        at(LAG["mix"], do_mix)
        for k in range(len(bits) + 1):
            @pl.when(t == pow_turn + k)
            def _(k=k):
                if k > 0:
                    pow_copy(k - 1).wait()
                    pow_sent[k] = pow_sent[k - 1] + pow_came[k - 1]
                if k < len(bits):
                    pow_copy(k).start()
        return 0

    lax.fori_loop(0, count + LAG["end"], turn_of, 0)

    total_count = rows * lax.axis_size("tensor") * CHUNK * per
    for n in range(2):
        total = jnp.sum(pow_sent[len(bits), n], keepdims=True)
        value = target[n] / jnp.sqrt(total / total_count + 1e-06)
        factor[n] = jnp.broadcast_to(value, factor.shape[1:])

    def drain(c, _):
        output(c).wait()
        return 0

    lax.fori_loop(0, count, drain, 0)


def local(old_weight, old_first, old_second, mixing, target_rms):
    rows, columns = old_weight.shape[1:]
    per = columns // CHUNK
    n = 3 * per
    w = CHUNK // PLANES
    hbm = pl.BlockSpec(memory_space=pl.ANY)
    smem = pl.BlockSpec(memory_space=pltpu.SMEM)

    def buf(k):
        return pltpu.VMEM((n, k, rows, w), F32)

    def pair(k):
        return pltpu.VMEM((n, k, 2, rows, w), F32)

    mixed, factor = pl.pallas_call(
        kernel,
        out_shape=(
            jax.ShapeDtypeStruct((3, 2, rows, columns), F32),
            jax.ShapeDtypeStruct((2, 8, LANES), F32),
        ),
        in_specs=[hbm, hbm, hbm, smem, smem],
        out_specs=(hbm, pl.BlockSpec(memory_space=pltpu.VMEM)),
        scratch_shapes=[
            pltpu.VMEM((n, rows, CHUNK), F32),
            buf(8), buf(5), buf(4), buf(3), buf(2), buf(5), buf(4), buf(3), buf(2),
            pair(8), pair(8), pair(8), pair(4),
            pltpu.VMEM((n, 2, rows, CHUNK), F32),
            pltpu.VMEM((5, 2, 8, LANES), F32), pltpu.VMEM((4, 2, 8, LANES), F32),
            pltpu.SemaphoreType.DMA((n,)), pltpu.SemaphoreType.DMA((n,)),
            pltpu.SemaphoreType.DMA((n, 17)), pltpu.SemaphoreType.DMA((n, 17)),
            pltpu.SemaphoreType.DMA((4,)), pltpu.SemaphoreType.DMA((4,)),
        ],
        compiler_params=pltpu.CompilerParams(
            collective_id=0, has_side_effects=True, vmem_limit_bytes=48 << 20),
        name="grow",
    )(old_weight, old_first, old_second, mixing, target_rms)
    scale = factor[:, :1, :1]
    return (scale * mixed[0], scale * mixed[1], scale * scale * mixed[2])


def solution(mesh):
    split = P("section", "tensor", None)
    return jax.shard_map(
        local,
        mesh=mesh,
        in_specs=(split, split, split, P(), P("section")),
        out_specs=(split, split, split),
        check_vma=False,
    )
```

time: 378 us -> 147 us (0.39)
  waiting for transfers between devices: 298 us -> 0 us
  Pallas kernels: 0 us -> 140 us
  blocking collectives: 29.6 us -> 0 us
  matrix products: 29.5 us -> 0 us
  between operations: 13.8 us -> 0.64 us
    all_gather x3 -> x0, waiting for transfers between devices: 296 us -> none  [the longest x1 118 us: local(): lax.all_gather(old_weight, 'section', axis=0, tiled=True)]
    pallas_call x0 -> x1, Pallas kernels: none -> 140 us  [local(): pl.pallas_call(kernel, out_shape=(jax.ShapeDtypeStruct((3, 2, rows, colum...]
    psum x1 -> x0, blocking collectives: 29.6 us -> none  [local(): power = lax.psum(local_power, 'tensor')]
    dot_general x3 -> x0, matrix products: 29.5 us -> none  [apply_coefs(): jnp.einsum('nl,lrd->nrd', coefs, stack, precision=lax.Precision.HIGHEST,...]
  transfers between devices with their start and end apart: 3 -> 0, of which waited for: 3 -> 0; matrix products, arithmetic and copies ran while one was open for 6% -> 0% of each run, Pallas kernels for 0% -> 0%
where the time goes in v1:
time: 147 us; the launch traced here: 146 us
  Pallas kernels  140 us (95%)
  local copies, waits for them, and re-layouts  4.41 us (3%)
  other arithmetic  1.63 us (1%)
    pallas_call x1, Pallas kernels, local(): pl.pallas_call(kernel, out_shape=(jax.ShapeDtypeStruct((3, 2, rows, colum...  140 us
    unnamed x9, local copies, waits for them, and re-layouts  4.41 us

profile of v1, /device:TPU:2, one launch (start us, length us, event | category | flops | bytes accessed | tf_op | source)
XLA Modules:
  0.0 146.2 jit_solution(6422777478596850373)
XLA Ops:
  0.6 0.8 copy.9.mixing
  1.4 0.0 copy-start
  1.4 1.0 copy-done
  2.4 0.0 copy-start.1
  2.4 1.0 copy-done.1
  3.4 0.0 copy-start.2
  3.4 1.0 copy-done.2
  4.4 0.0 copy-start.3
  4.4 0.7 copy-done.3
  5.0 139.5 %grow.1 = (f32[3,2,16,6144]{3,2,1,0:T(8,128)S(1)}, f32[2,8,128]{2,1,0:T(8,128)S(1)}) custom-call(f32[1,16,6144]{2,1,0:T(8,128)S(1)} %copy-done, f32[1,16,6144]{2,1,0:T(8,128)S(1)} %copy-done.1, f32[1,16,6144]{2,1,0:T(8,128)S(1)} %copy-done.2, f32[32,16]{1,0:T(8,128)S(1)} %copy.9.mixing, f32[2]{0:T(128)S(1)} %copy-done.3), custom_call_target="tpu_custom_call" | custom-call | tf_op jit(solution)/shard_map/grow/pallas_call | solution.py:265
  144.6 0.1 multiply_reduce_fusion
  144.7 1.5 %bitcast_multiply_fusion.1 = (f32[2,16,6144]{2,1,0:T(8,128)}, f32[2,16,6144]{2,1,0:T(8,128)}, f32[2,16,6144]{2,1,0:T(8,128)}) fusion(f32[3,2,16,6144]{3,2,1,0:T(8,128)S(1)} %get-tuple-element.6, f32[2]{0:T(128)S(1)} %get-tuple-element.8, f32[2]{0:T(128)S(1)} %get-tuple-element.7), kind=kLoop, calls=%fused_computation.1 | loop fusion | flops 589824 | bytes 4718608 | tf_op jit(solution)/shard_map/mul | solution.py:288
Async XLA Ops:
  1.4 1.0 copy-start
  2.4 1.0 copy-start.1
  3.4 1.0 copy-start.2
  4.4 0.7 copy-start.3

commit v2 on v0

v2 whole, which is shorter than its diff:
```python
import jax
import jax.numpy as jnp
from jax import lax
from jax.experimental import pallas as pl
from jax.experimental.pallas import tpu as pltpu
from jax.sharding import PartitionSpec as P

MESH = pl.DeviceIdType.MESH
F32 = jnp.float32
PLANES = 8
LANES = 128

HUBS = 2
CHUNK = 1024
LEAD = 2
POW_LAG = 2
LAGS = (3, 6, 9, 12)


def plan(hubs):
    arm = (PLANES - hubs) // 2
    last = hubs - 1
    sizes = [hubs - s + arm for s in range(1, hubs + 1)]
    firsts = [(last + arm - (hubs - 2), hubs, 0, 1), (arm - 1, hubs, sizes[0] + arm - 1, -1)]
    for j in range(1, arm):
        firsts.append((last + arm + 1 + j, 1, hubs - 1 + j, 1 + j))
        firsts.append((arm - 1 - j, 1, sizes[0] + arm - 1 - j, -1 - j))
    passes = []
    for s in range(1, hubs):
        n = sizes[s]
        passes.append(((1, 0, n, 1), (sizes[s - 1], n, n, -1)))
    sources = []
    for h in range(hubs):
        found = [("own", last + arm - h, 0)]
        for s in range(1, h + 1):
            found.append((s - 1, last - h, -s))
        for j in range(arm):
            found.append((h, hubs - h - 1 + j, -(h + 1 + j)))
        for s in range(1, hubs - h):
            found.append((s - 1, sizes[s - 1] + arm + hubs - s - 1 - h, s))
        for j in range(arm):
            found.append((last - h, sizes[last - h] + arm - 1 - j, hubs + j - h))
        sources.append(found)
    targets = []
    for j in range(arm, -1, -1):
        targets += [(0, -j), (last, j)]
    targets += [(h, 0) for h in range(1, last)]
    finished = {}
    for place, (hub, step) in enumerate(targets):
        finished[(hub + step) % PLANES] = ("part" if step == 0 else "back", place)
    return arm, sizes, firsts, passes, sources, targets, finished


def kernel(weight, first, second, mixing_in, target_in, mixed, factor, mixing, target, found, stage, own, *rest):
    arm, sizes, firsts, passes, sources, targets, finished = plan(HUBS)
    rl, rest = rest[:HUBS], rest[HUBS:]
    (part, sent, came, back, done, pow_sent, pow_came,
     load_sem, out_sem, ssem, rsem, pow_ssem, pow_rsem) = rest
    count, _, rows, width = own.shape
    per = count // 3
    section = lax.axis_index("section")
    tensor = lax.axis_index("tensor")
    z = section // 2
    half = lax.rem(section, 2)

    def plane(step):
        return lax.rem(z + (step + PLANES), PLANES)

    def along(step):
        return (plane(step) * 2 + half, tensor)

    def flip(bit):
        return (section, tensor + bit - 2 * bit * lax.rem(tensor // bit, 2))

    across = (z * 2 + 1 - half, tensor)
    partners = [flip(bit) for bit in (1, 8, 2, 4)]

    loads = [pltpu.make_async_copy(array.at[0], stage.at[a], load_sem.at[a])
             for a, array in enumerate((weight, first, second))]
    loads.append(pltpu.make_async_copy(mixing_in, mixing, load_sem.at[3]))
    loads.append(pltpu.make_async_copy(target_in, target, load_sem.at[4]))
    for load in loads:
        load.start()

    barrier = pltpu.get_barrier_semaphore()
    peers = [along(way * step) for step in range(1, arm + 1) for way in (1, -1)] + [across] + partners
    for peer in peers:
        pl.semaphore_signal(barrier, inc=1, device_id=peer, device_id_type=MESH)
    for load in loads:
        load.wait()

    def remote(src, dst, c, k, device):
        return pltpu.make_async_remote_copy(
            src_ref=src, dst_ref=dst, send_sem=ssem.at[k], recv_sem=rsem.at[c, k],
            device_id=device, device_id_type=MESH)

    def landed(c, k, ref):
        pltpu.make_async_copy(ref.at[c], ref.at[c], rsem.at[c, k]).wait()

    def left(k, ref):
        pltpu.make_async_copy(ref, ref, ssem.at[k]).wait()

    def turn(c):
        a = c // per
        start = lax.rem(c, per) * CHUNK
        for i in range(PLANES):
            slab = plane(i - (HUBS + arm - 1))
            own[c, i] = stage[a, :, pl.ds(pl.multiple_of(start + slab * width, LANES), width)]

    def do_first(c):
        for at, n, to, step in firsts:
            remote(own.at[c, pl.ds(at, n)], rl[0].at[c, pl.ds(to, n)], c, 0, along(step)).start()

    def do_pass(s, c):
        landed(c, s - 1, rl[s - 1])
        for at, to, n, step in passes[s - 1]:
            remote(rl[s - 1].at[c, pl.ds(at, n)], rl[s].at[c, pl.ds(to, n)], c, s, along(step)).start()

    def mix(c, place):
        squared = c >= 2 * per
        hub, step = targets[place]
        to = plane(step) * 2
        coefs = []
        for _, _, away in sources[hub]:
            layer = plane(away) * 2 + half
            for new in (2 * (to + half), 2 * (to + 1 - half)):
                for n in range(2):
                    coef = mixing[layer, new + n]
                    coefs.append(coef * jnp.where(squared, coef, 1.0))
        for lane in range(0, width, LANES):
            lanes = pl.ds(lane, LANES)
            sums = [None] * 4
            for i, (name, at, _) in enumerate(sources[hub]):
                old = (own if name == "own" else rl[name])[c, at, :, lanes]
                for n in range(4):
                    term = coefs[4 * i + n] * old
                    sums[n] = term if i == 0 else sums[n] + term
            for n in range(2):
                part[c, place, n, :, lanes] = sums[n]
                sent[c, place, n, :, lanes] = sums[2 + n]

    def do_mix(c):
        landed(c, HUBS - 1, rl[HUBS - 1])
        for at in (0, 4):
            for place in range(at, at + 4):
                mix(c, place)
            remote(sent.at[c, pl.ds(at, 4)], came.at[c, pl.ds(at, 4)], c, HUBS, across).start()

    def do_join(c):
        landed(c, HUBS, came)
        for i in range(2 * arm):
            part[c, i] = part[c, i] + came[c, i]
            remote(part.at[c, i], back.at[c, i], c, HUBS + 1, along(targets[i][1])).start()
        for i in range(2 * arm, PLANES):
            part[c, i] = part[c, i] + came[c, i]

    def output(c):
        s = lax.rem(c, per)
        return pltpu.make_async_copy(
            done.at[c], mixed.at[c // per, :, :, pl.ds(pl.multiple_of(s * CHUNK, CHUNK), CHUNK)], out_sem.at[0])

    def power(c):
        for n in range(2):
            total = pow_sent[0, n]
            for lane in range(0, CHUNK, LANES):
                for row in range(0, rows, 8):
                    value = done[c, n, pl.ds(row, 8), pl.ds(lane, LANES)]
                    total = total + value * value
            pow_sent[0, n] = total

    def do_end(c):
        landed(c, HUBS + 1, back)
        for role in range(PLANES):
            slab = plane(-role)
            lanes = pl.ds(pl.multiple_of(slab * width, LANES), width)
            name, at = finished[role]
            done[c, :, :, lanes] = (part if name == "part" else back)[c, at]
        output(c).start()

        @pl.when(c < per)
        def _():
            power(c)

    def pow_copy(k):
        return pltpu.make_async_remote_copy(
            src_ref=pow_sent.at[k], dst_ref=pow_came.at[k], send_sem=pow_ssem.at[k], recv_sem=pow_rsem.at[k],
            device_id=partners[k], device_id_type=MESH)

    factor_copy = pltpu.make_async_copy(found, factor, load_sem.at[5])

    def do_factor():
        total_count = rows * lax.axis_size("tensor") * CHUNK * per
        for n in range(2):
            total = jnp.sum(pow_sent[len(partners), n], keepdims=True)
            value = 1.0 / jnp.sqrt(total / total_count + 1e-06)
            scale = target[n] * value[0, 0]
            found[0, n] = scale
            found[1, n] = scale * scale
        factor_copy.start()

    pow_sent[0] = jnp.zeros_like(pow_sent[0])
    for c in range(LEAD):
        turn(c)
    pl.semaphore_wait(barrier, len(peers))
    for c in range(LEAD):
        do_first(c)

    pow_turn = LAGS[-1] + per - 1
    turns = max(count + LAGS[-1], pow_turn + POW_LAG * len(partners) + 1)

    def do_start(c):
        turn(c)
        do_first(c)

    steps = [(-LEAD, do_start)]
    for s in range(1, HUBS):
        steps.append((LAGS[s - 1], lambda c, s=s: do_pass(s, c)))
    steps += [(LAGS[-2], do_join), (LAGS[-1], do_end), (LAGS[-3], do_mix)]

    def turn_of(t, _):
        for lag, step in steps:
            c = t - lag

            @pl.when((c >= 0) & (c < count))
            def _(c=c, step=step):
                step(c)

        for k in range(len(partners) + 1):
            @pl.when(t == pow_turn + POW_LAG * k)
            def _(k=k):
                if k > 0:
                    pow_copy(k - 1).wait()
                    pow_sent[k] = pow_sent[k - 1] + pow_came[k - 1]
                if k < len(partners):
                    pow_copy(k).start()
                else:
                    do_factor()
        return 0

    lax.fori_loop(0, turns, turn_of, 0)

    for k, ref in enumerate((*rl, came, back)):
        left(k, ref)
    pltpu.make_async_copy(done, done, out_sem.at[0]).wait()
    factor_copy.wait()


def local(old_weight, old_first, old_second, mixing, target_rms):
    rows, columns = old_weight.shape[1:]
    n = 3 * columns // CHUNK
    w = CHUNK // PLANES
    arm, sizes = plan(HUBS)[:2]
    hbm = pl.BlockSpec(memory_space=pltpu.HBM)
    dma = pltpu.SemaphoreType.DMA

    def buf(k):
        return pltpu.VMEM((n, k, rows, w), F32)

    def pair(k):
        return pltpu.VMEM((n, k, 2, rows, w), F32)

    mixed, factor = pl.pallas_call(
        kernel,
        out_shape=(
            jax.ShapeDtypeStruct((3, 2, rows, columns), F32),
            jax.ShapeDtypeStruct((2, 2), F32),
        ),
        in_specs=[hbm] * 5,
        out_specs=(pl.BlockSpec(memory_space=pl.ANY), pl.BlockSpec(memory_space=pl.ANY)),
        scratch_shapes=[
            pltpu.SMEM(mixing.shape[::-1], F32), pltpu.SMEM(target_rms.shape, F32), pltpu.SMEM((2, 2), F32),
            pltpu.VMEM((3, rows, columns), F32), buf(PLANES), *[buf(2 * size) for size in sizes],
            pair(PLANES), pair(PLANES), pair(PLANES), pair(2 * arm),
            pltpu.VMEM((n, 2, rows, CHUNK), F32),
            pltpu.VMEM((5, 2, 8, LANES), F32), pltpu.VMEM((4, 2, 8, LANES), F32),
            dma((6,)), dma((1,)), dma((HUBS + 2,)), dma((n, HUBS + 2)), dma((4,)), dma((4,)),
        ],
        compiler_params=pltpu.CompilerParams(
            collective_id=0, has_side_effects=True, vmem_limit_bytes=60 << 20),
        name="grow",
    )(old_weight, old_first, old_second, mixing.T, target_rms)
    scale = factor[0][:, None, None]
    square = factor[1][:, None, None]
    return (scale * mixed[0], scale * mixed[1], square * mixed[2])


def solution(mesh):
    split = P("section", "tensor", None)
    return jax.shard_map(
        local,
        mesh=mesh,
        in_specs=(split, split, split, P(), P("section")),
        out_specs=(split, split, split),
        check_vma=False,
    )
```

time: 378 us -> 85.4 us (0.23)
  waiting for transfers between devices: 298 us -> 0 us
  Pallas kernels: 0 us -> 80.8 us
  blocking collectives: 29.6 us -> 0 us
  matrix products: 29.5 us -> 0 us
  between operations: 13.8 us -> 0.64 us
    all_gather x3 -> x0, waiting for transfers between devices: 296 us -> none  [the longest x1 118 us: local(): lax.all_gather(old_weight, 'section', axis=0, tiled=True)]
    pallas_call x0 -> x1, Pallas kernels: none -> 80.8 us  [local(): pl.pallas_call(kernel, out_shape=(jax.ShapeDtypeStruct((3, 2, rows, colum...]
    psum x1 -> x0, blocking collectives: 29.6 us -> none  [local(): power = lax.psum(local_power, 'tensor')]
    dot_general x3 -> x0, matrix products: 29.5 us -> none  [apply_coefs(): jnp.einsum('nl,lrd->nrd', coefs, stack, precision=lax.Precision.HIGHEST,...]
    unnamed x8 -> x0, local copies, waits for them, and re-layouts: 4.11 us -> none
  transfers between devices with their start and end apart: 3 -> 0, of which waited for: 3 -> 0; matrix products, arithmetic and copies ran while one was open for 6% -> 0% of each run, Pallas kernels for 0% -> 0%
where the time goes in v2:
time: 85.4 us; the launch traced here: 85.3 us
  Pallas kernels  80.8 us (95%)
  other arithmetic  3.12 us (4%)
    pallas_call x1, Pallas kernels, local(): pl.pallas_call(kernel, out_shape=(jax.ShapeDtypeStruct((3, 2, rows, colum...  80.8 us
    mul x1, other arithmetic, local(): return (scale * mixed[0], scale * mixed[1], square * mixed[2])  3.12 us

profile of v2, /device:TPU:2, one launch (start us, length us, event | category | flops | bytes accessed | tf_op | source)
XLA Modules:
  0.0 85.3 jit_solution(13596473702790727483)
XLA Ops:
  0.6 80.8 %grow.1 = (f32[3,2,16,6144]{3,2,1,0:T(8,128)}, f32[2,2]{1,0:T(2,128)}) custom-call(f32[1,16,6144]{2,1,0:T(8,128)} %weight.1, f32[1,16,6144]{2,1,0:T(8,128)} %first.1, f32[1,16,6144]{2,1,0:T(8,128)} %second.1, f32[16,32]{1,0:T(8,128)} %bitcast.11, f32[2]{0:T(128)} %target_in.1), custom_call_target="tpu_custom_call" | custom-call | tf_op jit(solution)/shard_map/grow/pallas_call | solution.py:262
  81.4 0.7 slice_bitcast_fusion
  82.2 3.1 %bitcast_multiply_fusion.1 = (f32[2,16,6144]{2,1,0:T(8,128)}, f32[2,16,6144]{2,1,0:T(8,128)}, f32[2,16,6144]{2,1,0:T(8,128)}) fusion(f32[3,2,16,6144]{3,2,1,0:T(8,128)} %get-tuple-element.6, f32[2]{0:T(128)S(1)} %get-tuple-element.11, f32[2]{0:T(128)S(1)} %get-tuple-element.10), kind=kLoop, calls=%fused_computation.1 | loop fusion | flops 589824 | bytes 4718608 | tf_op jit(solution)/shard_map/mul | solution.py:284

commit v3 on v2

v3 whole, which is shorter than its diff:
```python
import jax
import jax.numpy as jnp
from jax import lax
from jax.experimental import pallas as pl
from jax.experimental.pallas import tpu as pltpu
from jax.sharding import PartitionSpec as P

MESH = pl.DeviceIdType.MESH
F32 = jnp.float32
PLANES = 8
LANES = 128

GROUPS = ((2, 1024, 18, 0, (3, 6, 9, 12)),)
ORDER = ("first", "pass", "join", "end", "mix")
LEAD = 2
POW_LAG = 2


def plan(hubs):
    arm = (PLANES - hubs) // 2
    last = hubs - 1
    sizes = [hubs - s + arm for s in range(1, hubs + 1)]
    firsts = [(last + arm - (hubs - 2), hubs, 0, 1), (arm - 1, hubs, sizes[0] + arm - 1, -1)]
    for j in range(1, arm):
        firsts.append((last + arm + 1 + j, 1, hubs - 1 + j, 1 + j))
        firsts.append((arm - 1 - j, 1, sizes[0] + arm - 1 - j, -1 - j))
    passes = []
    for s in range(1, hubs):
        n = sizes[s]
        passes.append(((1, 0, n, 1), (sizes[s - 1], n, n, -1)))
    sources = []
    for h in range(hubs):
        found = [("own", last + arm - h, 0)]
        for s in range(1, h + 1):
            found.append((s - 1, last - h, -s))
        for j in range(arm):
            found.append((h, hubs - h - 1 + j, -(h + 1 + j)))
        for s in range(1, hubs - h):
            found.append((s - 1, sizes[s - 1] + arm + hubs - s - 1 - h, s))
        for j in range(arm):
            found.append((last - h, sizes[last - h] + arm - 1 - j, hubs + j - h))
        sources.append(found)
    targets = []
    for j in range(arm, -1, -1):
        targets += [(0, -j), (last, j)]
    targets += [(h, 0) for h in range(1, last)]
    finished = {}
    for place, (hub, step) in enumerate(targets):
        finished[(hub + step) % PLANES] = ("part" if step == 0 else "back", place)
    return arm, sizes, firsts, passes, sources, targets, finished


class Group:
    def __init__(self, spec, start, columns, refs, sems):
        self.hubs, self.chunk, self.count, self.base, self.lags = spec
        self.start, self.columns = start, columns
        self.width = self.chunk // PLANES
        (self.arm, self.sizes, self.firsts, self.passes, self.sources, self.targets,
         self.finished) = plan(self.hubs)
        self.own, self.part, self.sent, self.came, self.back, *self.rl = refs
        self.ssem, self.rsem = sems

    def where(self, c):
        at = self.start + c * self.chunk
        return at // self.columns, pl.multiple_of(lax.rem(at, self.columns), LANES)

    def landed(self, c, k, ref):
        pltpu.make_async_copy(ref.at[c], ref.at[c], self.rsem.at[c, k]).wait()


def kernel(*refs):
    (weight, first, second, mixing_in, target_in, mixed, factor, mixing, target, found,
     stage, done, pow_sent, pow_came, load_sem, out_sem, pow_ssem, pow_rsem), refs = refs[:18], refs[18:]
    _, rows, columns = stage.shape
    groups = []
    start = 0
    for spec in GROUPS:
        n = 5 + spec[0]
        groups.append(Group(spec, start, columns, refs[:n], refs[n:n + 2]))
        refs = refs[n + 2:]
        start += spec[1] * spec[2]
    section = lax.axis_index("section")
    tensor = lax.axis_index("tensor")
    z = section // 2
    half = lax.rem(section, 2)

    def plane(step):
        return lax.rem(z + (step + PLANES), PLANES)

    def along(step):
        return (plane(step) * 2 + half, tensor)

    def flip(bit):
        return (section, tensor + bit - 2 * bit * lax.rem(tensor // bit, 2))

    across = (z * 2 + 1 - half, tensor)
    partners = [flip(bit) for bit in (1, 8, 2, 4)]

    loads = [pltpu.make_async_copy(array.at[0], stage.at[a], load_sem.at[a])
             for a, array in enumerate((weight, first, second))]
    loads.append(pltpu.make_async_copy(mixing_in, mixing, load_sem.at[3]))
    loads.append(pltpu.make_async_copy(target_in, target, load_sem.at[4]))
    for load in loads:
        load.start()

    barrier = pltpu.get_barrier_semaphore()
    reach = max(group.arm for group in groups)
    peers = [along(way * step) for step in range(1, reach + 1) for way in (1, -1)] + [across] + partners
    for peer in peers:
        pl.semaphore_signal(barrier, inc=1, device_id=peer, device_id_type=MESH)

    def remote(g, src, dst, c, k, device):
        return pltpu.make_async_remote_copy(
            src_ref=src, dst_ref=dst, send_sem=g.ssem.at[k], recv_sem=g.rsem.at[c, k],
            device_id=device, device_id_type=MESH)

    def turn(g, c):
        a, col = g.where(c)
        for i in range(PLANES):
            slab = plane(i - (g.hubs + g.arm - 1))
            g.own[c, i] = stage[a, :, pl.ds(pl.multiple_of(col + slab * g.width, LANES), g.width)]

    def do_first(g, c):
        for at, n, to, step in g.firsts:
            remote(g, g.own.at[c, pl.ds(at, n)], g.rl[0].at[c, pl.ds(to, n)], c, 0, along(step)).start()

    def do_start(g, c):
        turn(g, c)
        do_first(g, c)

    def do_pass(s, g, c):
        g.landed(c, s - 1, g.rl[s - 1])
        for at, to, n, step in g.passes[s - 1]:
            remote(g, g.rl[s - 1].at[c, pl.ds(at, n)], g.rl[s].at[c, pl.ds(to, n)], c, s, along(step)).start()

    def mix(g, c, place):
        squared = g.where(c)[0] == 2
        hub, step = g.targets[place]
        to = plane(step) * 2
        coefs = []
        for _, _, away in g.sources[hub]:
            layer = plane(away) * 2 + half
            for new in (2 * (to + half), 2 * (to + 1 - half)):
                for n in range(2):
                    coef = mixing[layer, new + n]
                    coefs.append(coef * jnp.where(squared, coef, 1.0))
        for lane in range(0, g.width, LANES):
            lanes = pl.ds(lane, LANES)
            sums = [None] * 4
            for i, (name, at, _) in enumerate(g.sources[hub]):
                old = (g.own if name == "own" else g.rl[name])[c, at, :, lanes]
                for n in range(4):
                    term = coefs[4 * i + n] * old
                    sums[n] = term if i == 0 else sums[n] + term
            for n in range(2):
                g.part[c, place, n, :, lanes] = sums[n]
                g.sent[c, place, n, :, lanes] = sums[2 + n]

    def do_mix(g, c):
        g.landed(c, g.hubs - 1, g.rl[g.hubs - 1])
        for at in (0, 4):
            for place in range(at, at + 4):
                mix(g, c, place)
            remote(g, g.sent.at[c, pl.ds(at, 4)], g.came.at[c, pl.ds(at, 4)], c, g.hubs, across).start()

    def do_join(g, c):
        g.landed(c, g.hubs, g.came)
        for i in range(2 * g.arm):
            g.part[c, i] = g.part[c, i] + g.came[c, i]
            remote(g, g.part.at[c, i], g.back.at[c, i], c, g.hubs + 1, along(g.targets[i][1])).start()
        for i in range(2 * g.arm, PLANES):
            g.part[c, i] = g.part[c, i] + g.came[c, i]

    def do_end(g, c):
        g.landed(c, g.hubs + 1, g.back)
        a, col = g.where(c)
        for role in range(PLANES):
            slab = plane(-role)
            lanes = pl.ds(pl.multiple_of(col + slab * g.width, LANES), g.width)
            name, at = g.finished[role]
            done[a, :, :, lanes] = (g.part if name == "part" else g.back)[c, at]
        lanes = pl.ds(col, g.chunk)
        pltpu.make_async_copy(done.at[a, :, :, lanes], mixed.at[a, :, :, lanes], out_sem.at[0]).start()

        @pl.when(a == 0)
        def _():
            for n in range(2):
                total = pow_sent[0, n]
                for lane in range(0, g.chunk, LANES):
                    for row in range(0, rows, 8):
                        value = done[0, n, pl.ds(row, 8), pl.ds(pl.multiple_of(col + lane, LANES), LANES)]
                        total = total + value * value
                pow_sent[0, n] = total

    def pow_copy(k):
        return pltpu.make_async_remote_copy(
            src_ref=pow_sent.at[k], dst_ref=pow_came.at[k], send_sem=pow_ssem.at[k], recv_sem=pow_rsem.at[k],
            device_id=partners[k], device_id_type=MESH)

    factor_copy = pltpu.make_async_copy(found, factor, load_sem.at[5])

    def do_factor():
        total_count = rows * lax.axis_size("tensor") * columns
        for n in range(2):
            total = jnp.sum(pow_sent[len(partners), n], keepdims=True)
            value = 1.0 / jnp.sqrt(total / total_count + 1e-06)
            scale = target[n] * value[0, 0]
            found[0, n] = scale
            found[1, n] = scale * scale
        factor_copy.start()

    pow_sent[0] = jnp.zeros_like(pow_sent[0])
    loads[0].wait()
    for c in range(LEAD):
        turn(groups[0], c)
    pl.semaphore_wait(barrier, len(peers))
    for c in range(LEAD):
        do_first(groups[0], c)
    for load in loads[1:]:
        load.wait()

    steps = []
    for kind in ORDER:
        for i, g in enumerate(groups):
            if kind == "first":
                steps.append((g, g.base - LEAD, 0 if i else LEAD, do_start))
            elif kind == "pass":
                for s in range(1, g.hubs):
                    steps.append((g, g.base + g.lags[s - 1], 0, lambda g, c, s=s: do_pass(s, g, c)))
            else:
                at, step = {"mix": (-3, do_mix), "join": (-2, do_join), "end": (-1, do_end)}[kind]
                steps.append((g, g.base + g.lags[at], 0, step))
    pow_turn = max(g.base + g.lags[-1] + min(g.count, (columns - g.start) // g.chunk) - 1
                   for g in groups if g.start < columns)
    turns = max([g.base + g.lags[-1] + g.count for g in groups] + [pow_turn + POW_LAG * len(partners) + 1])

    def turn_of(t, _):
        for g, lag, least, step in steps:
            c = t - lag

            @pl.when((c >= least) & (c < g.count))
            def _(g=g, c=c, step=step):
                step(g, c)

        for k in range(len(partners) + 1):
            @pl.when(t == pow_turn + POW_LAG * k)
            def _(k=k):
                if k > 0:
                    pow_copy(k - 1).wait()
                    pow_sent[k] = pow_sent[k - 1] + pow_came[k - 1]
                if k < len(partners):
                    pow_copy(k).start()
                else:
                    do_factor()
        return 0

    lax.fori_loop(0, turns, turn_of, 0)

    for g in groups:
        for k, ref in enumerate((*g.rl, g.came, g.back)):
            pltpu.make_async_copy(ref, ref, g.ssem.at[k]).wait()
    pltpu.make_async_copy(done, done, out_sem.at[0]).wait()
    factor_copy.wait()


def scaled(factor_in, mixed, new_weight, new_first, new_second, factor, held, factor_sem, in_sem, out_sem):
    factor_copy = pltpu.make_async_copy(factor_in, factor, factor_sem.at[0])
    factor_copy.start()
    parts = [(a, n) for a in range(3) for n in range(2)]
    for a, n in parts:
        pltpu.make_async_copy(mixed.at[a, n], held.at[a, n], in_sem.at[a, n]).start()
    factor_copy.wait()
    outs = (new_weight, new_first, new_second)
    for a, n in parts:
        pltpu.make_async_copy(mixed.at[a, n], held.at[a, n], in_sem.at[a, n]).wait()
        scale = factor[1 if a == 2 else 0, n]
        held[a, n] = held[a, n] * scale
        pltpu.make_async_copy(held.at[a, n], outs[a].at[n], out_sem.at[a, n]).start()
    for a, n in parts:
        pltpu.make_async_copy(held.at[a, n], outs[a].at[n], out_sem.at[a, n]).wait()


def local(old_weight, old_first, old_second, mixing, target_rms):
    rows, columns = old_weight.shape[1:]
    hbm = pl.BlockSpec(memory_space=pltpu.HBM)
    dma = pltpu.SemaphoreType.DMA
    scratch = []
    for hubs, chunk, n, _, _ in GROUPS:
        arm, sizes = plan(hubs)[:2]
        w = chunk // PLANES
        for k in (PLANES,):
            scratch.append(pltpu.VMEM((n, k, rows, w), F32))
        for k in (PLANES, PLANES, PLANES, 2 * arm):
            scratch.append(pltpu.VMEM((n, k, 2, rows, w), F32))
        for size in sizes:
            scratch.append(pltpu.VMEM((n, 2 * size, rows, w), F32))
        scratch += [dma((hubs + 2,)), dma((n, hubs + 2))]
    mixed, factor = pl.pallas_call(
        kernel,
        out_shape=(
            jax.ShapeDtypeStruct((3, 2, rows, columns), F32),
            jax.ShapeDtypeStruct((2, 2), F32),
        ),
        in_specs=[hbm] * 5,
        out_specs=(hbm, hbm),
        scratch_shapes=[
            pltpu.SMEM(mixing.shape[::-1], F32), pltpu.SMEM(target_rms.shape, F32), pltpu.SMEM((2, 2), F32),
            pltpu.VMEM((3, rows, columns), F32), pltpu.VMEM((3, 2, rows, columns), F32),
            pltpu.VMEM((5, 2, 8, LANES), F32), pltpu.VMEM((4, 2, 8, LANES), F32),
            dma((6,)), dma((1,)), dma((4,)), dma((4,)), *scratch,
        ],
        compiler_params=pltpu.CompilerParams(
            collective_id=0, has_side_effects=True, vmem_limit_bytes=60 << 20),
        name="grow",
    )(old_weight, old_first, old_second, mixing.T, target_rms)
    new = jax.ShapeDtypeStruct((2, rows, columns), F32)
    return pl.pallas_call(
        scaled,
        out_shape=(new, new, new),
        in_specs=[hbm, hbm],
        out_specs=(hbm, hbm, hbm),
        scratch_shapes=[
            pltpu.SMEM((2, 2), F32), pltpu.VMEM((3, 2, rows, columns), F32),
            dma((1,)), dma((3, 2)), dma((3, 2)),
        ],
        compiler_params=pltpu.CompilerParams(vmem_limit_bytes=60 << 20),
        name="scale",
    )(factor, mixed)


def solution(mesh):
    split = P("section", "tensor", None)
    return jax.shard_map(
        local,
        mesh=mesh,
        in_specs=(split, split, split, P(), P("section")),
        out_specs=(split, split, split),
        check_vma=False,
    )
```

time: 85.4 us -> 84.1 us (0.985)
  other arithmetic: 3.12 us -> 0 us
  Pallas kernels: 80.8 us -> 83.3 us
    mul x1 -> x0, other arithmetic: 3.12 us -> none  [local(): return (scale * mixed[0], scale * mixed[1], square * mixed[2])]
    pallas_call x0 -> x1, Pallas kernels: none -> 2.53 us  [local(): pl.pallas_call(scaled, out_shape=(new, new, new), in_specs=[hbm, hbm], ou...]
where the time goes in v3:
time: 84.1 us; the launch traced here: 84 us
  Pallas kernels  83.3 us (99%)
    pallas_call x1, Pallas kernels, local(): pl.pallas_call(kernel, out_shape=(jax.ShapeDtypeStruct((3, 2, rows, colum...  80.8 us
    pallas_call x1, Pallas kernels, local(): pl.pallas_call(scaled, out_shape=(new, new, new), in_specs=[hbm, hbm], ou...  2.53 us

profile of v3, /device:TPU:2, one launch (start us, length us, event | category | flops | bytes accessed | tf_op | source)
XLA Modules:
  0.0 84.0 jit_solution(17332347257251087444)
XLA Ops:
  0.6 80.8 %grow.1 = (f32[3,2,16,6144]{3,2,1,0:T(8,128)}, f32[2,2]{1,0:T(2,128)}) custom-call(f32[1,16,6144]{2,1,0:T(8,128)} %refs_0_.1, f32[1,16,6144]{2,1,0:T(8,128)} %refs_1_.1, f32[1,16,6144]{2,1,0:T(8,128)} %refs_2_.1, f32[16,32]{1,0:T(8,128)} %bitcast.1, f32[2]{0:T(128)} %refs_4_.1), custom_call_target="tpu_custom_call" | custom-call | tf_op jit(solution)/shard_map/grow/pallas_call | solution.py:298
  81.4 2.5 %scale.1 = (f32[2,16,6144]{2,1,0:T(8,128)}, f32[2,16,6144]{2,1,0:T(8,128)}, f32[2,16,6144]{2,1,0:T(8,128)}) custom-call(f32[2,2]{1,0:T(2,128)} %get-tuple-element.5.factor_in, f32[3,2,16,6144]{3,2,1,0:T(8,128)} %get-tuple-element.6.mixed), custom_call_target="tpu_custom_call" | custom-call | tf_op jit(solution)/shard_map/scale/pallas_call | solution.py:317

commit v4 on v3

--- a/solution.py
+++ b/solution.py
@@ -10,53 +10,59 @@
 PLANES = 8
 LANES = 128
 
-GROUPS = ((2, 1024, 18, 0, (3, 6, 9, 12)),)
+GROUPS = (
+    (2, 3, 1024, 16, 0, (3, 6, 9, 12), 1),
+    (4, 2, 1024, 2, 0, (3, 6, 9, 12, 15, 18), 5),
+)
 ORDER = ("first", "pass", "join", "end", "mix")
 LEAD = 2
 POW_LAG = 2
 
 
-def plan(hubs):
-    arm = (PLANES - hubs) // 2
+def plan(hubs, before):
+    after = PLANES - hubs - before
     last = hubs - 1
-    sizes = [hubs - s + arm for s in range(1, hubs + 1)]
-    firsts = [(last + arm - (hubs - 2), hubs, 0, 1), (arm - 1, hubs, sizes[0] + arm - 1, -1)]
-    for j in range(1, arm):
-        firsts.append((last + arm + 1 + j, 1, hubs - 1 + j, 1 + j))
-        firsts.append((arm - 1 - j, 1, sizes[0] + arm - 1 - j, -1 - j))
-    passes = []
-    for s in range(1, hubs):
-        n = sizes[s]
-        passes.append(((1, 0, n, 1), (sizes[s - 1], n, n, -1)))
+    right = [hubs - s + before for s in range(1, hubs + 1)]
+    left = [hubs - s + after for s in range(1, hubs + 1)]
+    firsts = [(after + 1, hubs, 0, 1), (after - 1, hubs, right[0] + after - 1, -1)]
+    for j in range(1, max(before, after)):
+        if j < before:
+            firsts.append((hubs + after + j, 1, last + j, 1 + j))
+        if j < after:
+            firsts.append((after - 1 - j, 1, right[0] + after - 1 - j, -1 - j))
+    passes = [((1, 0, right[s], 1), (right[s - 1], right[s], left[s], -1)) for s in range(1, hubs)]
     sources = []
     for h in range(hubs):
-        found = [("own", last + arm - h, 0)]
+        found = [("own", last + after - h, 0)]
         for s in range(1, h + 1):
             found.append((s - 1, last - h, -s))
-        for j in range(arm):
-            found.append((h, hubs - h - 1 + j, -(h + 1 + j)))
+        for j in range(before):
+            found.append((h, last - h + j, -(h + 1 + j)))
         for s in range(1, hubs - h):
-            found.append((s - 1, sizes[s - 1] + arm + hubs - s - 1 - h, s))
-        for j in range(arm):
-            found.append((last - h, sizes[last - h] + arm - 1 - j, hubs + j - h))
+            found.append((s - 1, right[s - 1] + after + last - s - h, s))
+        for j in range(after):
+            found.append((last - h, right[last - h] + after - 1 - j, hubs + j - h))
         sources.append(found)
     targets = []
-    for j in range(arm, -1, -1):
-        targets += [(0, -j), (last, j)]
-    targets += [(h, 0) for h in range(1, last)]
+    for j in range(max(before, after), 0, -1):
+        targets += [(0, -j)] * (j <= before) + [(last, j)] * (j <= after)
+    targets += [(0, 0), (last, 0)] + [(h, 0) for h in range(1, last)]
     finished = {}
     for place, (hub, step) in enumerate(targets):
         finished[(hub + step) % PLANES] = ("part" if step == 0 else "back", place)
-    return arm, sizes, firsts, passes, sources, targets, finished
+    sizes = [r + l for r, l in zip(right, left)]
+    return sizes, firsts, passes, sources, targets, finished
 
 
 class Group:
     def __init__(self, spec, start, columns, refs, sems):
-        self.hubs, self.chunk, self.count, self.base, self.lags = spec
+        self.hubs, self.before, self.chunk, self.count, self.base, self.lags, self.stride = spec
+        self.arms = PLANES - self.hubs
+        self.after = self.arms - self.before
         self.start, self.columns = start, columns
         self.width = self.chunk // PLANES
-        (self.arm, self.sizes, self.firsts, self.passes, self.sources, self.targets,
-         self.finished) = plan(self.hubs)
+        (_, self.firsts, self.passes, self.sources, self.targets,
+         self.finished) = plan(self.hubs, self.before)
         self.own, self.part, self.sent, self.came, self.back, *self.rl = refs
         self.ssem, self.rsem = sems
 
@@ -78,7 +84,7 @@
         n = 5 + spec[0]
         groups.append(Group(spec, start, columns, refs[:n], refs[n:n + 2]))
         refs = refs[n + 2:]
-        start += spec[1] * spec[2]
+        start += spec[2] * spec[3]
     section = lax.axis_index("section")
     tensor = lax.axis_index("tensor")
     z = section // 2
@@ -104,7 +110,7 @@
         load.start()
 
     barrier = pltpu.get_barrier_semaphore()
-    reach = max(group.arm for group in groups)
+    reach = max(max(group.before, group.after) for group in groups)
     peers = [along(way * step) for step in range(1, reach + 1) for way in (1, -1)] + [across] + partners
     for peer in peers:
         pl.semaphore_signal(barrier, inc=1, device_id=peer, device_id_type=MESH)
@@ -117,7 +123,7 @@
     def turn(g, c):
         a, col = g.where(c)
         for i in range(PLANES):
-            slab = plane(i - (g.hubs + g.arm - 1))
+            slab = plane(i - (g.hubs + g.after - 1))
             g.own[c, i] = stage[a, :, pl.ds(pl.multiple_of(col + slab * g.width, LANES), g.width)]
 
     def do_first(g, c):
@@ -165,10 +171,10 @@
 
     def do_join(g, c):
         g.landed(c, g.hubs, g.came)
-        for i in range(2 * g.arm):
+        for i in range(g.arms):
             g.part[c, i] = g.part[c, i] + g.came[c, i]
             remote(g, g.part.at[c, i], g.back.at[c, i], c, g.hubs + 1, along(g.targets[i][1])).start()
-        for i in range(2 * g.arm, PLANES):
+        for i in range(g.arms, PLANES):
             g.part[c, i] = g.part[c, i] + g.came[c, i]
 
     def do_end(g, c):
@@ -223,22 +229,25 @@
     for kind in ORDER:
         for i, g in enumerate(groups):
             if kind == "first":
-                steps.append((g, g.base - LEAD, 0 if i else LEAD, do_start))
+                steps.append((g, g.base - (0 if i else LEAD) * g.stride, 0 if i else LEAD, do_start))
             elif kind == "pass":
                 for s in range(1, g.hubs):
                     steps.append((g, g.base + g.lags[s - 1], 0, lambda g, c, s=s: do_pass(s, g, c)))
             else:
                 at, step = {"mix": (-3, do_mix), "join": (-2, do_join), "end": (-1, do_end)}[kind]
                 steps.append((g, g.base + g.lags[at], 0, step))
-    pow_turn = max(g.base + g.lags[-1] + min(g.count, (columns - g.start) // g.chunk) - 1
+    pow_turn = max(g.base + g.lags[-1] + (min(g.count, (columns - g.start) // g.chunk) - 1) * g.stride
                    for g in groups if g.start < columns)
-    turns = max([g.base + g.lags[-1] + g.count for g in groups] + [pow_turn + POW_LAG * len(partners) + 1])
+    turns = max([g.base + g.lags[-1] + (g.count - 1) * g.stride + 1 for g in groups] + [pow_turn + POW_LAG * len(partners) + 1])
 
     def turn_of(t, _):
         for g, lag, least, step in steps:
-            c = t - lag
-
-            @pl.when((c >= least) & (c < g.count))
+            c = (t - lag) // g.stride if g.stride > 1 else t - lag
+            on_turn = (t - lag >= 0) & (c >= least) & (c < g.count)
+            if g.stride > 1:
+                on_turn &= lax.rem(t - lag, g.stride) == 0
+
+            @pl.when(on_turn)
             def _(g=g, c=c, step=step):
                 step(g, c)
 
@@ -285,15 +294,15 @@
     hbm = pl.BlockSpec(memory_space=pltpu.HBM)
     dma = pltpu.SemaphoreType.DMA
     scratch = []
-    for hubs, chunk, n, _, _ in GROUPS:
-        arm, sizes = plan(hubs)[:2]
+    for hubs, before, chunk, n, _, _, _ in GROUPS:
+        sizes = plan(hubs, before)[0]
         w = chunk // PLANES
         for k in (PLANES,):
             scratch.append(pltpu.VMEM((n, k, rows, w), F32))
-        for k in (PLANES, PLANES, PLANES, 2 * arm):
+        for k in (PLANES, PLANES, PLANES, PLANES - hubs):
             scratch.append(pltpu.VMEM((n, k, 2, rows, w), F32))
         for size in sizes:
-            scratch.append(pltpu.VMEM((n, 2 * size, rows, w), F32))
+            scratch.append(pltpu.VMEM((n, size, rows, w), F32))
         scratch += [dma((hubs + 2,)), dma((n, hubs + 2))]
     mixed, factor = pl.pallas_call(
         kernel,

time: 84.1 us -> 83.9 us (level)
  no operation moved by 1% of the time
where the time goes in v4:
time: 83.9 us; the launch traced here: 83.7 us
  Pallas kernels  83.1 us (99%)
    pallas_call x1, Pallas kernels, local(): pl.pallas_call(kernel, out_shape=(jax.ShapeDtypeStruct((3, 2, rows, colum...  80.6 us
    pallas_call x1, Pallas kernels, local(): pl.pallas_call(scaled, out_shape=(new, new, new), in_specs=[hbm, hbm], ou...  2.53 us

profile of v4, /device:TPU:2, one launch (start us, length us, event | category | flops | bytes accessed | tf_op | source)
XLA Modules:
  0.0 83.7 jit_solution(7118765425243972164)
XLA Ops:
  0.6 80.6 %grow.1 = (f32[3,2,16,6144]{3,2,1,0:T(8,128)}, f32[2,2]{1,0:T(2,128)}) custom-call(f32[1,16,6144]{2,1,0:T(8,128)} %refs_0_.1, f32[1,16,6144]{2,1,0:T(8,128)} %refs_1_.1, f32[1,16,6144]{2,1,0:T(8,128)} %refs_2_.1, f32[16,32]{1,0:T(8,128)} %bitcast.1, f32[2]{0:T(128)} %refs_4_.1), custom_call_target="tpu_custom_call" | custom-call | tf_op jit(solution)/shard_map/grow/pallas_call | solution.py:307
  81.2 2.5 %scale.1 = (f32[2,16,6144]{2,1,0:T(8,128)}, f32[2,16,6144]{2,1,0:T(8,128)}, f32[2,16,6144]{2,1,0:T(8,128)}) custom-call(f32[2,2]{1,0:T(2,128)} %get-tuple-element.5.factor_in, f32[3,2,16,6144]{3,2,1,0:T(8,128)} %get-tuple-element.6.mixed), custom_call_target="tpu_custom_call" | custom-call | tf_op jit(solution)/shard_map/scale/pallas_call | solution.py:326

commit v5 on v4

--- a/solution.py
+++ b/solution.py
@@ -106,14 +106,13 @@
              for a, array in enumerate((weight, first, second))]
     loads.append(pltpu.make_async_copy(mixing_in, mixing, load_sem.at[3]))
     loads.append(pltpu.make_async_copy(target_in, target, load_sem.at[4]))
-    for load in loads:
-        load.start()
-
     barrier = pltpu.get_barrier_semaphore()
     reach = max(max(group.before, group.after) for group in groups)
     peers = [along(way * step) for step in range(1, reach + 1) for way in (1, -1)] + [across] + partners
     for peer in peers:
         pl.semaphore_signal(barrier, inc=1, device_id=peer, device_id_type=MESH)
+    for load in loads:
+        load.start()
 
     def remote(g, src, dst, c, k, device):
         return pltpu.make_async_remote_copy(

time: 83.9 us -> 83.9 us (level)
  no operation moved by 1% of the time
where the time goes in v5:
time: 83.9 us; the launch traced here: 83.7 us
  Pallas kernels  83.1 us (99%)
    pallas_call x1, Pallas kernels, local(): pl.pallas_call(kernel, out_shape=(jax.ShapeDtypeStruct((3, 2, rows, colum...  80.6 us
    pallas_call x1, Pallas kernels, local(): pl.pallas_call(scaled, out_shape=(new, new, new), in_specs=[hbm, hbm], ou...  2.53 us

profile of v5, /device:TPU:2, one launch (start us, length us, event | category | flops | bytes accessed | tf_op | source)
XLA Modules:
  0.0 83.7 jit_solution(14698300157767827650)
XLA Ops:
  0.6 80.6 %grow.1 = (f32[3,2,16,6144]{3,2,1,0:T(8,128)}, f32[2,2]{1,0:T(2,128)}) custom-call(f32[1,16,6144]{2,1,0:T(8,128)} %refs_0_.1, f32[1,16,6144]{2,1,0:T(8,128)} %refs_1_.1, f32[1,16,6144]{2,1,0:T(8,128)} %refs_2_.1, f32[16,32]{1,0:T(8,128)} %bitcast.1, f32[2]{0:T(128)} %refs_4_.1), custom_call_target="tpu_custom_call" | custom-call | tf_op jit(solution)/shard_map/grow/pallas_call | solution.py:306
  81.2 2.5 %scale.1 = (f32[2,16,6144]{2,1,0:T(8,128)}, f32[2,16,6144]{2,1,0:T(8,128)}, f32[2,16,6144]{2,1,0:T(8,128)}) custom-call(f32[2,2]{1,0:T(2,128)} %get-tuple-element.5.factor_in, f32[3,2,16,6144]{3,2,1,0:T(8,128)} %get-tuple-element.6.mixed), custom_call_target="tpu_custom_call" | custom-call | tf_op jit(solution)/shard_map/scale/pallas_call | solution.py:325
